TPU v7x, 256 devices: a whole 4x4x8 slice. The times are simulated.
256 devices in a mesh: crow: 16 (over y, x), ccol: 8 (over z), lvl: 2 (over core).
Axes of the slice: x: 4, y: 4, z: 8, core: 2. Of those that a mesh axis runs over, the one named last changes fastest.
Arguments:
- x_field: bfloat16 [16, 16, 2, 8, 256], P('crow', 'ccol', 'lvl'), may hold values from -6 to 6
- near_blocks: bfloat16 [16, 8, 2, 64, 256, 256], P('crow', 'ccol', 'lvl'), may hold values from -0.0625 to 0.0625
- near_pairs: int32 [16, 8, 2, 64, 2], P('crow', 'ccol', 'lvl'), may hold values from 0 to 63, as said below
- far_left: bfloat16 [16, 8, 2, 128, 32, 256], P('crow', 'ccol', 'lvl'), may hold values from -0.25 to 0.25
- far_right: bfloat16 [16, 8, 2, 128, 32, 256], P('crow', 'ccol', 'lvl'), may hold values from -0.25 to 0.25
- far_pairs: int32 [16, 8, 2, 128, 2], P('crow', 'ccol', 'lvl'), may hold values from 0 to 63, as said below
- tile_counts: int32 [16, 8, 2, 2], P('crow', 'ccol', 'lvl'), may hold values from 1 to 32, as said below
Outputs:
- product: float32 [16, 16, 2, 8, 256], P('crow', 'ccol', 'lvl')
Inputs may be any that keep to these rules, and one draw needn't show every extreme that they name: `near_pairs`: entry 0 is a row-set index below 32, entry 1 a column-set index below 64. `far_pairs`: entry 0 is a row-set index below 32, entry 1 a column-set index below 64. `tile_counts`: entry 0 is at most 16, entry 1 at most 32; some device has all its near slots live and some device all its far slots.
All inputs are finite; a program needn't handle non-finite values.
Results may differ from a plain program's by a relative error of at most 0.0024.
Values may be sent and summed in bfloat16 or wider, within the bound.
A program may use at most 64 MiB of HBM per device.

v0:
```python
import jax
import jax.numpy as jnp
from jax import lax
from jax.sharding import PartitionSpec as P

TILE = 4


def near_apply(state, arrays, pairs, row_set, col_set):
    row_acc, col_acc = state
    blocks = arrays[0]
    rows = pairs[:, 0]
    cols = pairs[:, 1]
    forward = jnp.einsum("pab,psb->psa", blocks, col_set[cols], preferred_element_type=jnp.float32)
    backward = jnp.einsum("pab,psa->psb", blocks, row_set[rows], preferred_element_type=jnp.float32)
    return (row_acc.at[rows].add(forward), col_acc.at[cols].add(backward))


def far_apply(state, arrays, pairs, row_set, col_set):
    row_acc, col_acc = state
    left, right = arrays
    rows = pairs[:, 0]
    cols = pairs[:, 1]
    coef_col = jnp.einsum(
        "pkb,psb->psk", right, col_set[cols], preferred_element_type=jnp.float32
    ).astype(jnp.bfloat16)
    coef_row = jnp.einsum(
        "pka,psa->psk", left, row_set[rows], preferred_element_type=jnp.float32
    ).astype(jnp.bfloat16)
    forward = jnp.einsum("pka,psk->psa", left, coef_col, preferred_element_type=jnp.float32)
    backward = jnp.einsum("pkb,psk->psb", right, coef_row, preferred_element_type=jnp.float32)
    return (row_acc.at[rows].add(forward), col_acc.at[cols].add(backward))


def run_tiles(state, arrays, pairs, first, last, offset, apply_fn, row_set, col_set):

    def one_tile(tile, carry):
        start = (tile - offset) * TILE
        pieces = tuple((lax.dynamic_slice_in_dim(item, start, TILE, 0) for item in arrays))
        tile_pairs = lax.dynamic_slice_in_dim(pairs, start, TILE, 0)
        return apply_fn(carry, pieces, tile_pairs, row_set, col_set)

    return lax.fori_loop(first, last, one_tile, state)


def per_device(x_field, near_blocks, near_pairs, far_left, far_right, far_pairs, tile_counts):
    per_dev = x_field.shape[1]
    rhs_count = x_field.shape[3]
    width = x_field.shape[4]
    n_row = lax.axis_size("crow")
    n_col = lax.axis_size("ccol")
    n_lvl = lax.axis_size("lvl")
    rank = far_left.shape[4]
    pieces = lax.all_gather(x_field, "lvl", axis=2, tiled=True)
    row_set = lax.all_gather(pieces, "ccol", axis=1, tiled=True).reshape(-1, rhs_count, width)
    col_set = lax.all_gather(pieces, "crow", axis=0, tiled=True).reshape(-1, rhs_count, width)
    near_slots = near_blocks.shape[3]
    far_slots = far_left.shape[3]
    blocks = near_blocks.reshape(near_slots, width, width)
    npairs = near_pairs.reshape(near_slots, 2)
    left = far_left.reshape(far_slots, rank, width)
    right = far_right.reshape(far_slots, rank, width)
    fpairs = far_pairs.reshape(far_slots, 2)
    counts = tile_counts.reshape(2)
    state = (jnp.zeros(row_set.shape, jnp.float32), jnp.zeros(col_set.shape, jnp.float32))
    state = run_tiles(state, (blocks,), npairs, 0, counts[0], 0, near_apply, row_set, col_set)
    state = run_tiles(state, (left, right), fpairs, 0, counts[1], 0, far_apply, row_set, col_set)
    row_acc = state[0].reshape(1, n_col * per_dev, n_lvl, rhs_count, width)
    col_acc = state[1].reshape(n_row, per_dev, n_lvl, rhs_count, width)
    row_part = lax.psum_scatter(row_acc, "ccol", scatter_dimension=1, tiled=True)
    col_part = lax.psum_scatter(col_acc, "crow", scatter_dimension=0, tiled=True)
    result = lax.psum_scatter(row_part + col_part, "lvl", scatter_dimension=2, tiled=True)
    return result


def solution(mesh):
    placed = (
        P("crow", "ccol", "lvl", None, None),
        P("crow", "ccol", "lvl", None, None, None),
        P("crow", "ccol", "lvl", None, None),
        P("crow", "ccol", "lvl", None, None, None),
        P("crow", "ccol", "lvl", None, None, None),
        P("crow", "ccol", "lvl", None, None),
        P("crow", "ccol", "lvl", None),
    )
    return jax.shard_map(
        per_device,
        mesh=mesh,
        in_specs=placed,
        out_specs=P("crow", "ccol", "lvl", None, None),
        check_vma=False,
    )
```

profile of v0, /device:TPU:1, one launch (start us, length us, event | category | flops | bytes accessed | tf_op | source)
XLA Modules:
  0.0 377.9 jit_solution(6971041648761489181)
XLA Ops:
  6.5 5.1 %all_gather.9 = bf16[1,2,2,8,256]{4,3,2,1,0:T(8,128)(2,1)S(1)} all-gather(bf16[1,2,1,8,256]{4,3,2,1,0:T(8,128)(2,1)} %param.11), channel_id=1, replica_groups=mesh['crow'=16,'ccol'=8,'lvl'=2] {'lvl'}, dimensions={2}, use_global_device_ids=true | all-gather | bytes 24576 | tf_op jit(solution)/shard_map/all_gather | solution.py:54
  11.7 17.2 %all_gather.10 = bf16[16,2,2,8,256]{4,3,2,1,0:T(8,128)(2,1)S(1)} all-gather(bf16[1,2,2,8,256]{4,3,2,1,0:T(8,128)(2,1)S(1)} %all_gather.9), channel_id=1, replica_groups=mesh['crow'=16,'ccol'=8,'lvl'=2] {'crow'}, dimensions={0}, use_global_device_ids=true | all-gather | bytes 278528 | tf_op jit(solution)/shard_map/all_gather | solution.py:56
  28.8 21.8 %all_gather.11 = bf16[1,16,2,8,256]{4,3,2,0,1:T(8,128)(2,1)S(1)} all-gather(bf16[1,2,2,8,256]{4,3,2,0,1:T(8,128)(2,1)S(1)} %bitcast.47), channel_id=1, replica_groups=mesh['crow'=16,'ccol'=8,'lvl'=2] {'ccol'}, dimensions={1}, use_global_device_ids=true | all-gather | bytes 147456 | tf_op jit(solution)/shard_map/all_gather | solution.py:55
  50.7 1.4 fusion.22
  52.1 13.2 %while.24 = (s32[]{:T(128)}, f32[32,8,256]{2,1,0:T(8,128)S(1)}, f32[64,8,256]{2,1,0:T(8,128)S(1)}, s32[]{:T(128)}, s32[64,2]{0,1:T(2,128)}, /*index=5*/bf16[64,8...) while((s32[]{:T(128)}, f32[32,8,256]{2,1,0:T(8,128)S(1)}, ...), condition=%wide.region_3.0_spmd, body=%wide.region_0.0_spmd.sunk | while | flops 8407070 | bytes 1417615 | solution.py:43
  54.1 1.2 fusion.49
  56.5 1.3 fusion.48
  60.4 1.2 fusion.49
  62.8 1.3 fusion.48
  65.3 121.0 %while.25 = (s32[]{:T(128)}, f32[32,8,256]{2,1,0:T(8,128)S(1)}, f32[64,8,256]{2,1,0:T(8,128)S(1)}, s32[]{:T(128)}, s32[128,2]{0,1:T(2,128)S(1)}, /*index=5*/bf16...) while((s32[]{:T(128)}, f32[32,8,256]{2,1,0:T(8,128)S(1)}, ...), condition=%wide.region_7.0_spmd, body=%wide.region_4.0_spmd.sunk | while | flops 2117662 | bytes 633231 | solution.py:43
  66.7 1.1 fusion.58
  69.0 1.1 fusion.57
  72.2 1.1 fusion.58
  74.5 1.1 fusion.57
  77.6 1.1 fusion.58
  80.0 1.1 fusion.57
  83.1 1.1 fusion.58
  85.4 1.1 fusion.57
  88.6 1.1 fusion.58
  90.9 1.1 fusion.57
  94.0 1.1 fusion.58
  96.4 1.1 fusion.57
  99.5 1.1 fusion.58
  101.8 1.1 fusion.57
  105.0 1.1 fusion.58
  107.3 1.1 fusion.57
  110.4 1.1 fusion.58
  112.8 1.1 fusion.57
  115.9 1.1 fusion.58
  118.2 1.1 fusion.57
  121.4 1.1 fusion.58
  123.7 1.1 fusion.57
  126.8 1.1 fusion.58
  129.2 1.1 fusion.57
  132.3 1.1 fusion.58
  134.6 1.1 fusion.57
  137.8 1.1 fusion.58
  140.1 1.1 fusion.57
  143.2 1.1 fusion.58
  145.6 1.1 fusion.57
  148.7 1.1 fusion.58
  151.0 1.1 fusion.57
  156.5 1.1 fusion.57
  181.5 1.1 fusion.58
  188.4 91.3 %reduce-scatter.6.cloned.1.call-done = f32[1,2,2,8,256]{4,3,2,1,0:T(8,128)} async-done(((f32[1,16,2,8,256]{4,3,2,1,0:T(8,128)}), f32[1,2,2,8,256]{4,3,2,1,0:T(8,128)}) %reduce-scatter.6.cloned.1.call-update) | async-done | bytes 32784 | tf_op jit(solution)/shard_map/reduce_scatter | solution.py:70
  279.8 83.8 %reduce-scatter.8.cloned.1.call-done = f32[1,2,2,8,256]{4,3,2,1,0:T(8,128)} async-done(((f32[16,2,2,8,256]{4,3,2,1,0:T(8,128)}), f32[1,2,2,8,256]{4,3,2,1,0:T(8,128)}) %reduce-scatter.8.cloned.1.call-update) | async-done | bytes 32784
  364.3 5.5 %all-reduce.1 = f32[1,2,2,8,256]{4,3,2,1,0:T(8,128)S(1)} all-reduce(f32[1,2,2,8,256]{4,3,2,1,0:T(8,128)S(1)} %add.52), channel_id=4, replica_groups=mesh['crow'=16,'ccol'=8,'lvl'=2] {'lvl'}, use_global_device_ids=true, to_apply=%region_10.0.clone | all-reduce | flops 8192 | bytes 65536
  369.9 1.2 constant_dynamic-slice_fusion.2
  (194 shorter events, 75.2 us)
Async XLA Ops:
  6.5 273.2 %reduce-scatter.6.cloned.1.call-start = ((), (), s32[]{:S(2)}) async-start(), calls=%async_computation.2 | async-start | bytes 294912 | tf_op jit(solution)/shard_map/reduce_scatter | solution.py:70
  52.1 13.2 %copy-start.2 = (s32[1,1,1,128,2]{3,4,2,1,0:T(2,128)S(1)}, s32[1,1,1,128,2]{3,4,2,1,0:T(2,128)}, u32[]{:S(2)}) copy-start(s32[1,1,1,128,2]{3,4,2,1,0:T(2,128)} %param.16) | copy-start | bytes 3076
  65.3 122.5 %copy-start.3 = (u32[256]{0:T(256)S(1)}, u32[256]{0:T(256)}, u32[]{:S(2)}) copy-start(u32[256]{0:T(256)} %constant.43) | copy-start | bytes 3076
  186.3 0.7 copy-start.1
  186.3 0.9 copy-start
  187.0 176.5 %reduce-scatter.8.cloned.1.call-start = ((), (), s32[]{:S(2)}) async-start(), calls=%async_computation.3 | async-start | bytes 557056
Sparse Core Ops, SparseCore 0:
  187.2 92.5 reduce-scatter.5
  283.6 79.8 reduce-scatter.7
where the time goes:
time: 382 us; the launch traced here: 378 us
  waiting for transfers between devices  176 us (46%)
  matrix products  54.1 us (14%)
  blocking collectives  49.6 us (13%)
  local copies, waits for them, and re-layouts  33.5 us (9%)
  other arithmetic  32.5 us (9%)
  loops' own time  18.8 us (5%)
  between operations  13.5 us (4%)
    reduce_scatter x1, waiting for transfers between devices, per_device(): lax.psum_scatter(row_acc, 'ccol', scatter_dimension=1, tiled=True)  91.3 us
    unnamed x3, waiting for transfers between devices  84.4 us
    scatter-add x44, other arithmetic, far_apply(): return (row_acc.at[rows].add(forward), col_acc.at[cols].add(backward))  28.7 us
    dot_general x22, matrix products, far_apply(): jnp.einsum('pka,psk->psa', left, coef_col, preferred_element_type=jnp.flo...  24.6 us
    dot_general x22, matrix products, far_apply(): jnp.einsum('pkb,psk->psb', right, coef_row, preferred_element_type=jnp.fl...  24.6 us
    all_gather x1, blocking collectives, per_device(): lax.all_gather(pieces, 'ccol', axis=1, tiled=True)  21.8 us
    another operation x2, loops' own time, run_tiles(): return lax.fori_loop(first, last, one_tile, state)  18.8 us
    all_gather x1, blocking collectives, per_device(): lax.all_gather(pieces, 'crow', axis=0, tiled=True)  17.2 us
  transfers between devices with their start and end apart: 2, of which 2 were waited for; matrix products, arithmetic and copies ran while one was open for 0% of the time, Pallas kernels for 0%

commit v1 on v0

v1 whole, which is shorter than its diff:
```python
import functools

import jax
import jax.numpy as jnp
from jax import lax
from jax.experimental import pallas as pl
from jax.experimental.pallas import tpu as pltpu
from jax.sharding import PartitionSpec as P

TILE = 4
GROUP = 8
F32 = jnp.float32
BF16 = jnp.bfloat16
NT = (((1,), (1,)), ((), ()))
MESH = pl.DeviceIdType.MESH


def swap_low(value):
    return (value & -4) | ((value & 1) << 1) | ((value >> 1) & 1)


def placement(pairs, count, sets, rhs):
    slots = pairs.shape[1]
    live = lax.broadcasted_iota(jnp.int32, (1, slots), 1) < count * TILE
    wide = slots * rhs
    spread = (
        lax.broadcasted_iota(jnp.int32, (slots, wide), 1) // rhs
        == lax.broadcasted_iota(jnp.int32, (slots, wide), 0)
    )
    spread = jnp.where(spread, 1.0, 0.0).astype(BF16)
    inner = lax.broadcasted_iota(jnp.int32, (1, wide), 1) % rhs
    out = []
    for which, total in enumerate(sets):
        index = swap_low(pairs[which : which + 1, :])
        index = jnp.where(live, index, -1).astype(F32).astype(BF16)
        index = jnp.broadcast_to(index, (8, slots))
        target = jnp.dot(index, spread, preferred_element_type=F32)[:1]
        target = target.astype(jnp.int32) * rhs + inner
        rows = lax.broadcasted_iota(jnp.int32, (total * rhs, wide), 0)
        out.append(jnp.where(rows == target, 1.0, 0.0).astype(BF16))
    return out


def kernel(
    n_row, n_col, n_lvl,
    x_hbm, near_hbm, left_hbm, right_hbm, np_hbm, fp_hbm, cnt_hbm,
    out_ref,
    x_ref, np_s, fp_s, cnt_s, np_v, fp_v,
    near, left, right, row_in, col_in, row_x, col_x, row_f, col_f,
    near_kr, near_kc, far_kr, far_kc,
    row_out, col_out, row_back, col_back,
    small_sem, block_sem, near_sem, gsend, grow, gcol, rsend, rrow, rcol,
):
    r, c, k = lax.axis_index("crow"), lax.axis_index("ccol"), lax.axis_index("lvl")
    rhs, width = 8, x_ref.shape[1]
    n_near, n_groups = near.shape[0], left.shape[0]
    near_step = n_near // near_sem.shape[0]
    rp, cp = n_col * n_lvl, n_row * n_lvl
    me_r, me_c = c * n_lvl + k, r * n_lvl + k

    small = [
        pltpu.make_async_copy(src, dst, small_sem.at[i])
        for i, (src, dst) in enumerate(
            ((x_hbm, x_ref), (np_hbm, np_v), (fp_hbm, fp_v), (cnt_hbm, cnt_s), (np_hbm, np_s), (fp_hbm, fp_s))
        )
    ]
    for copy in small:
        copy.start()
    far_copies = [
        pltpu.make_async_copy(left_hbm, left, block_sem.at[0]),
        pltpu.make_async_copy(right_hbm, right, block_sem.at[1]),
    ]
    for copy in far_copies:
        copy.start()

    def near_copy(step):
        part = pl.ds(step * near_step, near_step)
        return pltpu.make_async_copy(near_hbm.at[part], near.at[part], near_sem.at[step])

    for step in range(near_sem.shape[0]):
        near_copy(step).start()

    barrier = pltpu.get_barrier_semaphore()

    def row_peer(o):
        to = lax.rem(me_r + o, rp)
        return to, {"crow": r, "ccol": to // n_lvl, "lvl": lax.rem(to, n_lvl)}

    def col_peer(o):
        to = lax.rem(me_c + o, cp)
        return to, {"crow": to // n_lvl, "ccol": c, "lvl": lax.rem(to, n_lvl)}

    def greet(peer):
        def body(o, carry):
            pl.semaphore_signal(barrier, inc=1, device_id=peer(o)[1], device_id_type=MESH)
            return carry

        return body

    lax.fori_loop(1, rp, greet(row_peer), 0)
    lax.fori_loop(1, cp, greet(col_peer), 0)

    for copy in small:
        copy.wait()
    row_in[me_r] = x_ref[...]
    col_in[me_c] = x_ref[...]
    near_kr[...], near_kc[...] = placement(np_v[...], cnt_s[0], (2 * rp, 2 * cp), rhs)
    far_kr[...], far_kc[...] = placement(fp_v[...], cnt_s[1], (2 * rp, 2 * cp), rhs)

    pl.semaphore_wait(barrier, rp - 1 + cp - 1)

    def send_x(peer, buf, mine, sem):
        def body(o, carry):
            pltpu.make_async_remote_copy(
                src_ref=x_ref, dst_ref=buf.at[mine], send_sem=gsend, recv_sem=sem,
                device_id=peer(o)[1], device_id_type=MESH,
            ).start()
            return carry

        return body

    lax.fori_loop(1, rp, send_x(row_peer, row_in, me_r, grow), 0)
    lax.fori_loop(1, cp, send_x(col_peer, col_in, me_c, gcol), 0)

    def drain(buf, count, sem):
        part = buf.at[pl.ds(0, count)]
        pltpu.make_async_copy(part, part, sem).wait()

    drain(row_in, rp - 1, grow)
    drain(col_in, cp - 1, gcol)

    def unpack(src, dst):
        def body(a, carry):
            for kk in range(n_lvl):
                v = src[a * n_lvl + kk].astype(F32).reshape(2, rhs, width)
                for jj in range(2):
                    dst[a * 2 * n_lvl + jj * n_lvl + kk] = v[jj]
            return carry

        lax.fori_loop(0, src.shape[0] // n_lvl, body, 0)

    unpack(row_in, row_x)
    unpack(col_in, col_x)

    def near_body(step, carry):
        near_copy(step).wait()
        for u in range(near_step):
            slot = step * near_step + u
            block = near[slot]
            xp = row_x[np_s[0, slot]].astype(BF16)
            xq = col_x[np_s[1, slot]].astype(BF16)
            at = pl.ds(pl.multiple_of(slot * rhs, rhs), rhs)
            row_f[at] = lax.dot_general(xq, block, NT, preferred_element_type=F32)
            col_f[at] = jnp.dot(xp, block, preferred_element_type=F32)
        return carry

    lax.fori_loop(0, near_sem.shape[0], near_body, 0)

    for copy in far_copies:
        copy.wait()
    rank = width // GROUP
    diag = (
        lax.broadcasted_iota(jnp.int32, (GROUP * rhs, width), 0) // rhs
        == lax.broadcasted_iota(jnp.int32, (GROUP * rhs, width), 1) // rank
    )

    def far_body(g, carry):
        xp = jnp.concatenate([row_x[fp_s[0, g * GROUP + u]] for u in range(GROUP)], 0).astype(BF16)
        xq = jnp.concatenate([col_x[fp_s[1, g * GROUP + u]] for u in range(GROUP)], 0).astype(BF16)
        lg, rg = left[g], right[g]
        cq = lax.dot_general(xq, rg, NT, preferred_element_type=F32)
        cr = lax.dot_general(xp, lg, NT, preferred_element_type=F32)
        cq = jnp.where(diag, cq, 0.0).astype(BF16)
        cr = jnp.where(diag, cr, 0.0).astype(BF16)
        at = pl.ds(pl.multiple_of((n_near + g * GROUP) * rhs, GROUP * rhs), GROUP * rhs)
        row_f[at] = jnp.dot(cq, lg, preferred_element_type=F32)
        col_f[at] = jnp.dot(cr, rg, preferred_element_type=F32)
        return carry

    lax.fori_loop(0, n_groups, far_body, 0)

    def scatter(f, kn, kf, out):
        split = n_near * rhs

        def halves(part):
            v = f[part]
            hi = v.astype(BF16)
            return hi, (v - hi.astype(F32)).astype(BF16)

        total = None
        for kmat, part in ((kn, pl.ds(0, split)), (kf, pl.ds(split, f.shape[0] - split))):
            for half in halves(part):
                term = jnp.dot(kmat[...], half, preferred_element_type=F32)
                total = term if total is None else total + term
        out[...] = total.astype(BF16).reshape(out.shape)

    scatter(row_f, near_kr, far_kr, row_out)

    def send_back(peer, src, dst, mine, sem):
        def body(o, carry):
            to, where = peer(o)
            pltpu.make_async_remote_copy(
                src_ref=src.at[to], dst_ref=dst.at[mine], send_sem=rsend, recv_sem=sem,
                device_id=where, device_id_type=MESH,
            ).start()
            return carry

        return body

    lax.fori_loop(1, rp, send_back(row_peer, row_out, row_back, me_r, rrow), 0)
    scatter(col_f, near_kc, far_kc, col_out)
    lax.fori_loop(1, cp, send_back(col_peer, col_out, col_back, me_c, rcol), 0)

    row_back[me_r] = row_out[me_r]
    col_back[me_c] = col_out[me_c]
    drain(row_back, rp - 1, rrow)
    total = row_back[0].astype(F32)
    for a in range(1, rp):
        total = total + row_back[a].astype(F32)
    drain(col_back, cp - 1, rcol)
    for a in range(cp):
        total = total + col_back[a].astype(F32)
    out_ref[...] = total
    drain(row_in, rp - 1, gsend)
    drain(col_in, cp - 1, gsend)
    drain(row_back, rp - 1, rsend)
    drain(col_back, cp - 1, rsend)


def per_device(x_field, near_blocks, near_pairs, far_left, far_right, far_pairs, tile_counts):
    n_row, n_col, n_lvl = (lax.axis_size(a) for a in ("crow", "ccol", "lvl"))
    per, rhs, width = x_field.shape[1], x_field.shape[3], x_field.shape[4]
    n_near, n_far, rank = near_blocks.shape[3], far_left.shape[3], far_left.shape[4]
    n_groups = n_far // GROUP
    x = x_field.reshape(per * rhs, width)
    near = near_blocks.reshape(n_near, width, width)
    left = far_left.reshape(n_groups, GROUP * rank, width)
    right = far_right.reshape(n_groups, GROUP * rank, width)
    npairs = near_pairs.reshape(n_near, 2).T
    fpairs = far_pairs.reshape(n_far, 2).T
    counts = tile_counts.reshape(2)
    rp, cp = n_col * n_lvl, n_row * n_lvl
    rows, cols = per * rp, per * cp
    slots = n_near + n_far
    vmem = pl.BlockSpec(memory_space=pltpu.VMEM)
    hbm = pl.BlockSpec(memory_space=pltpu.HBM)
    dma = pltpu.SemaphoreType.DMA
    out = pl.pallas_call(
        functools.partial(kernel, n_row, n_col, n_lvl),
        out_shape=jax.ShapeDtypeStruct((per * rhs, width), F32),
        in_specs=[hbm] * 7,
        out_specs=vmem,
        scratch_shapes=[
            pltpu.VMEM(x.shape, BF16),
            pltpu.SMEM(npairs.shape, jnp.int32),
            pltpu.SMEM(fpairs.shape, jnp.int32),
            pltpu.SMEM(counts.shape, jnp.int32),
            pltpu.VMEM(npairs.shape, jnp.int32),
            pltpu.VMEM(fpairs.shape, jnp.int32),
            pltpu.VMEM(near.shape, BF16),
            pltpu.VMEM(left.shape, BF16),
            pltpu.VMEM(right.shape, BF16),
            pltpu.VMEM((rp, per * rhs, width), BF16),
            pltpu.VMEM((cp, per * rhs, width), BF16),
            pltpu.VMEM((rows, rhs, width), F32),
            pltpu.VMEM((cols, rhs, width), F32),
            pltpu.VMEM((slots * rhs, width), F32),
            pltpu.VMEM((slots * rhs, width), F32),
            pltpu.VMEM((rows * rhs, n_near * rhs), BF16),
            pltpu.VMEM((cols * rhs, n_near * rhs), BF16),
            pltpu.VMEM((rows * rhs, n_far * rhs), BF16),
            pltpu.VMEM((cols * rhs, n_far * rhs), BF16),
            pltpu.VMEM((rp, per * rhs, width), BF16),
            pltpu.VMEM((cp, per * rhs, width), BF16),
            pltpu.VMEM((rp, per * rhs, width), BF16),
            pltpu.VMEM((cp, per * rhs, width), BF16),
            dma((6,)),
            dma((2,)),
            dma((8,)),
            dma, dma, dma, dma, dma, dma,
        ],
        compiler_params=pltpu.CompilerParams(
            collective_id=0, has_side_effects=True, vmem_limit_bytes=56 * 1024 * 1024
        ),
        cost_estimate=pl.CostEstimate(
            flops=4 * slots * rhs * width * width,
            bytes_accessed=2 * (near.size + left.size + right.size),
            transcendentals=0,
        ),
    )(x, near, left, right, npairs, fpairs, counts)
    return out.reshape(x_field.shape)


def solution(mesh):
    placed = (
        P("crow", "ccol", "lvl", None, None),
        P("crow", "ccol", "lvl", None, None, None),
        P("crow", "ccol", "lvl", None, None),
        P("crow", "ccol", "lvl", None, None, None),
        P("crow", "ccol", "lvl", None, None, None),
        P("crow", "ccol", "lvl", None, None),
        P("crow", "ccol", "lvl", None),
    )
    return jax.shard_map(
        per_device,
        mesh=mesh,
        in_specs=placed,
        out_specs=P("crow", "ccol", "lvl", None, None),
        check_vma=False,
    )
```

time: 382 us -> 37.9 us (0.10); the launches traced: 378 us -> 37.7 us
  waiting for transfers between devices: 176 us -> 0 us
  matrix products: 54.1 us -> 0 us
  blocking collectives: 49.6 us -> 0 us
  Pallas kernels: 0 us -> 36.4 us
  other arithmetic: 32.5 us -> 0 us
  local copies, waits for them, and re-layouts: 33.5 us -> 1.32 us
  loops' own time: 18.8 us -> 0 us
  between operations: 13.5 us -> 0.01 us
    reduce_scatter x1 -> x0, waiting for transfers between devices: 91.3 us -> none  [per_device(): lax.psum_scatter(row_acc, 'ccol', scatter_dimension=1, tiled=True)]
    unnamed x3 -> x0, waiting for transfers between devices: 84.4 us -> none
    dot_general x48 -> x0, matrix products: 54.1 us -> none  [the longest x22 24.6 us: far_apply(): jnp.einsum('pka,psk->psa', left, coef_col, preferred_element_type=jnp.flo...]
    all_gather x3 -> x0, blocking collectives: 44.1 us -> none  [the longest x1 21.8 us: per_device(): lax.all_gather(pieces, 'ccol', axis=1, tiled=True)]
    pallas_call x0 -> x1, Pallas kernels: none -> 36.4 us  [per_device(): pl.pallas_call(functools.partial(kernel, n_row, n_col, n_lvl), out_shape=...]
    scatter-add x48 -> x0, other arithmetic: 31.4 us -> none  [the longest x44 28.7 us: far_apply(): return (row_acc.at[rows].add(forward), col_acc.at[cols].add(backward))]
    gather x48 -> x0, local copies, waits for them, and re-layouts: 26.3 us -> none  [the longest x22 12.1 us: far_apply(): col_set[cols]]
    another operation x2 -> x0, loops' own time: 18.8 us -> none  [run_tiles(): return lax.fori_loop(first, last, one_tile, state)]
  transfers between devices with their start and end apart: 2 -> 0, of which waited for: 2 -> 0; matrix products, arithmetic and copies ran while one was open for 0% -> 0% of each run, Pallas kernels for 0% -> 0%
where the time goes in v1:
time: 37.9 us; the launch traced here: 37.7 us
  Pallas kernels  36.4 us (96%)
  local copies, waits for them, and re-layouts  1.32 us (3%)
    pallas_call x1, Pallas kernels, per_device(): pl.pallas_call(functools.partial(kernel, n_row, n_col, n_lvl), out_shape=...  36.4 us
    unnamed x1, local copies, waits for them, and re-layouts  1.32 us

profile of v1, /device:TPU:1, one launch (start us, length us, event | category | flops | bytes accessed | tf_op | source)
XLA Modules:
  0.0 37.7 jit_solution(1937493609751756987)
XLA Ops:
  0.0 36.4 %shard_map.73 = f32[16,256]{1,0:T(8,128)} custom-call(bf16[16,256]{1,0:T(8,128)(2,1)} %bitcast.18, bf16[64,256,256]{2,1,0:T(8,128)(2,1)} %bitcast.14, bf16[16,256,256]{2,1,0:T(8,128)(2,1)} %bitcast.15, bf16[16,256,256]{2,1,0:T(8,128)(2,1)} %bitcast.16, s32[2,64]{1,0:T(2,128)} %bitcast.19, s32[2,128]{1,0:T(2,128)} %bitcast.20, s32[2]{0:T(128)} %bitcast.21), custom_call_target="tpu_custom_call" | custom-call | flops 402653184 | bytes 12582912 | tf_op jit(solution)/shard_map/pallas_call | solution.py:248
  36.4 1.3 %copy.10 = f32[1,2,1,8,256]{4,3,2,1,0:T(8,128)} copy(f32[1,2,1,8,256]{4,3,2,1,0:T(8,128)} %bitcast.17) | data formatting | bytes 32768

commit v2 on v1

v2 whole, which is shorter than its diff:
```python
import functools

import jax
import jax.numpy as jnp
from jax import lax
from jax.experimental import pallas as pl
from jax.experimental.pallas import tpu as pltpu
from jax.sharding import PartitionSpec as P

TILE = 4
GROUP = 8
UNROLL = 32
F32 = jnp.float32
BF16 = jnp.bfloat16
MESH = pl.DeviceIdType.MESH


def far_first(n):
    return sorted(range(n), key=lambda o: -min(o, n - o))


def chain_tables(pairs, count, which):
    slots = pairs.shape[1]
    by_lane = jnp.broadcast_to(pairs[which : which + 1, :], (slots, slots)).astype(F32)
    by_row = by_lane.T
    t = lax.broadcasted_iota(jnp.int32, (slots, slots), 0)
    s = lax.broadcasted_iota(jnp.int32, (slots, slots), 1)
    before = (by_row == by_lane) & (t < s)
    prev = jnp.max(jnp.where(before, t + 1, 0), axis=0, keepdims=True)
    mine = (by_row == s.astype(F32)) & (t < count * TILE)
    last = jnp.max(jnp.where(mine, t + 1, 0), axis=0, keepdims=True)
    return prev, last


def kernel(
    n_row, n_col, n_lvl,
    x_hbm, near_hbm, left_hbm, right_hbm, np_hbm, fp_hbm, cnt_hbm,
    out_ref,
    x_ref, np_s, fp_s, cnt_s, np_v, fp_v, tab_v, tab_s,
    near, left, right, near_t, left_t, right_t,
    row_in, col_in, row_x, col_x, row_n, row_f, col_n, col_f,
    row_out, col_out, row_back, col_back,
    small_sem, far_sem, near_sem, tab_sem, gsend, grow, gcol, rsend, rrow, rcol,
):
    r, c, k = lax.axis_index("crow"), lax.axis_index("ccol"), lax.axis_index("lvl")
    rhs, width = 8, x_ref.shape[1]
    n_near, n_groups = near.shape[0], left.shape[0]
    n_far = n_groups * GROUP
    rank = width // GROUP
    near_step = n_near // near_sem.shape[0]
    rp, cp = n_col * n_lvl, n_row * n_lvl
    me_r, me_c = c * n_lvl + k, r * n_lvl + k

    nx = 4 if n_row % 4 == 0 else n_row
    ny = n_row // nx
    y, x = r // nx, lax.rem(r, nx)
    zs = [c] + [lax.rem(c + o, n_col) for o in range(1, n_col)]
    ys = [y] + [lax.rem(y + o, ny) for o in range(1, ny)]
    xs = [x] + [lax.rem(x + o, nx) for o in range(1, nx)]
    ks = [k] + [lax.rem(k + o, n_lvl) for o in range(1, n_lvl)]
    row_peers, col_peers = [], []
    for oz in far_first(n_col):
        for ok in range(n_lvl):
            if oz or ok:
                row_peers.append((zs[oz] * n_lvl + ks[ok], {"crow": r, "ccol": zs[oz], "lvl": ks[ok]}))
    grid = [(oy, ox) for oy in range(ny) for ox in range(nx)]
    grid.sort(key=lambda o: -min(o[0], ny - o[0]) - min(o[1], nx - o[1]))
    for oy, ox in grid:
        to = ys[oy] * nx + xs[ox]
        for ok in range(n_lvl):
            if oy or ox or ok:
                col_peers.append((to * n_lvl + ks[ok], {"crow": to, "ccol": c, "lvl": ks[ok]}))

    barrier = pltpu.get_barrier_semaphore()
    for _, where in row_peers + col_peers:
        pl.semaphore_signal(barrier, inc=1, device_id=where, device_id_type=MESH)

    small = [
        pltpu.make_async_copy(src, dst, small_sem.at[i])
        for i, (src, dst) in enumerate(
            ((x_hbm, x_ref), (np_hbm, np_v), (fp_hbm, fp_v), (cnt_hbm, cnt_s), (np_hbm, np_s), (fp_hbm, fp_s))
        )
    ]
    for copy in small:
        copy.start()
    far_copies = [
        pltpu.make_async_copy(left_hbm, left, far_sem.at[0]),
        pltpu.make_async_copy(right_hbm, right, far_sem.at[1]),
    ]

    def near_copy(step):
        part = pl.ds(step * near_step, near_step)
        return pltpu.make_async_copy(near_hbm.at[part], near.at[part], near_sem.at[step])

    for copy in far_copies:
        copy.start()
    for step in range(near_sem.shape[0]):
        near_copy(step).start()

    small[0].wait()
    pl.semaphore_wait(barrier, rp - 1 + cp - 1)
    for peers, buf, mine, sem in ((row_peers, row_in, me_r, grow), (col_peers, col_in, me_c, gcol)):
        for _, where in peers:
            pltpu.make_async_remote_copy(
                src_ref=x_ref, dst_ref=buf.at[mine], send_sem=gsend, recv_sem=sem,
                device_id=where, device_id_type=MESH,
            ).start()

    row_in[me_r] = x_ref[...]
    col_in[me_c] = x_ref[...]
    for copy in small[1:]:
        copy.wait()
    tab_v[...] = jnp.zeros_like(tab_v)
    zero = jnp.zeros((rhs, width), F32)
    for total in (row_n, row_f, col_n, col_f):
        total[0] = zero
    for pairs, count, at in ((np_v, 0, 0), (fp_v, 1, 2)):
        slots = pairs.shape[1]
        for which in range(2):
            prev, last = chain_tables(pairs[...], cnt_s[count], which)
            tab_v[at + which : at + which + 1, :slots] = prev
            tab_v[4 + at + which : 5 + at + which, :slots] = last
    tab_copy = pltpu.make_async_copy(tab_v, tab_s, tab_sem)
    tab_copy.start()

    for copy in far_copies:
        copy.wait()

    def far_turn(g, carry):
        left_t[g] = left[g].T
        right_t[g] = right[g].T
        return carry

    lax.fori_loop(0, n_groups, far_turn, 0)

    def near_turn(step, carry):
        near_copy(step).wait()
        for u in range(near_step):
            slot = step * near_step + u
            near_t[slot] = near[slot].T
        return carry

    lax.fori_loop(0, near_sem.shape[0], near_turn, 0)
    tab_copy.wait()

    def drain(buf, count, sem):
        part = buf.at[pl.ds(0, count)]
        pltpu.make_async_copy(part, part, sem).wait()

    def unpack(src, dst):
        def body(a, carry):
            for kk in range(n_lvl):
                v = src[a * n_lvl + kk].astype(F32).reshape(2, rhs, width)
                for jj in range(2):
                    dst[a * 2 * n_lvl + jj * n_lvl + kk] = v[jj]
            return carry

        lax.fori_loop(0, src.shape[0] // n_lvl, body, 0)

    diag = (
        lax.broadcasted_iota(jnp.int32, (GROUP * rhs, width), 0) // rhs
        == lax.broadcasted_iota(jnp.int32, (GROUP * rhs, width), 1) // rank
    )
    far_u = UNROLL * n_groups // n_near

    def one_way(field, side, blocks, first, second, near_sum, far_sum, chain):
        def body(step, carry):
            for u in range(UNROLL):
                slot = step * UNROLL + u
                v = field[np_s[side, slot]].astype(BF16)
                part = jnp.dot(v, blocks[slot], preferred_element_type=F32)
                near_sum[slot + 1] = part + near_sum[tab_s[chain, slot]]
            for u in range(far_u):
                g = step * far_u + u
                v = jnp.concatenate([field[fp_s[side, g * GROUP + w]] for w in range(GROUP)], 0)
                coef = jnp.dot(v.astype(BF16), first[g], preferred_element_type=F32)
                coef = jnp.where(diag, coef, 0.0).astype(BF16)
                part = jnp.dot(coef, second[g], preferred_element_type=F32)
                for w in range(GROUP):
                    slot = g * GROUP + w
                    far_sum[slot + 1] = part[w * rhs : (w + 1) * rhs] + far_sum[tab_s[2 + chain, slot]]
            return carry

        lax.fori_loop(0, n_near // UNROLL, body, 0)

    def collect(near_sum, far_sum, chain, out):
        def body(a, carry):
            for kk in range(n_lvl):
                parts = []
                for jj in range(2):
                    p = a * 2 * n_lvl + jj * n_lvl + kk
                    parts.append(near_sum[tab_s[4 + chain, p]] + far_sum[tab_s[6 + chain, p]])
                out[a * n_lvl + kk] = jnp.concatenate(parts, 0).astype(BF16)
            return carry

        lax.fori_loop(0, out.shape[0] // n_lvl, body, 0)

    def send_back(peers, src, dst, mine, sem):
        for to, where in peers:
            pltpu.make_async_remote_copy(
                src_ref=src.at[to], dst_ref=dst.at[mine], send_sem=rsend, recv_sem=sem,
                device_id=where, device_id_type=MESH,
            ).start()

    drain(row_in, rp - 1, grow)
    unpack(row_in, row_x)
    one_way(row_x, 0, near, left_t, right, col_n, col_f, 1)
    collect(col_n, col_f, 1, col_out)
    send_back(col_peers, col_out, col_back, me_c, rcol)

    drain(col_in, cp - 1, gcol)
    unpack(col_in, col_x)
    one_way(col_x, 1, near_t, right_t, left, row_n, row_f, 0)
    collect(row_n, row_f, 0, row_out)
    send_back(row_peers, row_out, row_back, me_r, rrow)

    col_back[me_c] = col_out[me_c]
    row_back[me_r] = row_out[me_r]
    drain(col_back, cp - 1, rcol)
    total = col_back[0].astype(F32)
    for a in range(1, cp):
        total = total + col_back[a].astype(F32)
    drain(row_back, rp - 1, rrow)
    for a in range(rp):
        total = total + row_back[a].astype(F32)
    out_ref[...] = total
    drain(row_in, rp - 1, gsend)
    drain(col_in, cp - 1, gsend)
    drain(row_back, rp - 1, rsend)
    drain(col_back, cp - 1, rsend)


def per_device(x_field, near_blocks, near_pairs, far_left, far_right, far_pairs, tile_counts):
    n_row, n_col, n_lvl = (lax.axis_size(a) for a in ("crow", "ccol", "lvl"))
    per, rhs, width = x_field.shape[1], x_field.shape[3], x_field.shape[4]
    n_near, n_far, rank = near_blocks.shape[3], far_left.shape[3], far_left.shape[4]
    n_groups = n_far // GROUP
    x = x_field.reshape(per * rhs, width)
    near = near_blocks.reshape(n_near, width, width)
    left = far_left.reshape(n_groups, GROUP * rank, width)
    right = far_right.reshape(n_groups, GROUP * rank, width)
    npairs = near_pairs.reshape(n_near, 2).T
    fpairs = far_pairs.reshape(n_far, 2).T
    counts = tile_counts.reshape(2)
    rp, cp = n_col * n_lvl, n_row * n_lvl
    rows, cols = per * rp, per * cp
    vmem = pl.BlockSpec(memory_space=pltpu.VMEM)
    hbm = pl.BlockSpec(memory_space=pltpu.HBM)
    dma = pltpu.SemaphoreType.DMA
    operands = [
        pltpu.with_memory_space_constraint(a, pltpu.HBM)
        for a in (x, near, left, right, npairs, fpairs, counts)
    ]
    out = pl.pallas_call(
        functools.partial(kernel, n_row, n_col, n_lvl),
        out_shape=jax.ShapeDtypeStruct((per * rhs, width), F32),
        in_specs=[hbm] * 7,
        out_specs=vmem,
        scratch_shapes=[
            pltpu.VMEM(x.shape, BF16),
            pltpu.SMEM(npairs.shape, jnp.int32),
            pltpu.SMEM(fpairs.shape, jnp.int32),
            pltpu.SMEM(counts.shape, jnp.int32),
            pltpu.VMEM(npairs.shape, jnp.int32),
            pltpu.VMEM(fpairs.shape, jnp.int32),
            pltpu.VMEM((8, 128), jnp.int32),
            pltpu.SMEM((8, 128), jnp.int32),
            pltpu.VMEM(near.shape, BF16),
            pltpu.VMEM(left.shape, BF16),
            pltpu.VMEM(right.shape, BF16),
            pltpu.VMEM(near.shape, BF16),
            pltpu.VMEM(left.shape, BF16),
            pltpu.VMEM(right.shape, BF16),
            pltpu.VMEM((rp, per * rhs, width), BF16),
            pltpu.VMEM((cp, per * rhs, width), BF16),
            pltpu.VMEM((rows, rhs, width), F32),
            pltpu.VMEM((cols, rhs, width), F32),
            pltpu.VMEM((n_near + 1, rhs, width), F32),
            pltpu.VMEM((n_far + 1, rhs, width), F32),
            pltpu.VMEM((n_near + 1, rhs, width), F32),
            pltpu.VMEM((n_far + 1, rhs, width), F32),
            pltpu.VMEM((rp, per * rhs, width), BF16),
            pltpu.VMEM((cp, per * rhs, width), BF16),
            pltpu.VMEM((rp, per * rhs, width), BF16),
            pltpu.VMEM((cp, per * rhs, width), BF16),
            dma((6,)),
            dma((2,)),
            dma((8,)),
            dma, dma, dma, dma, dma, dma, dma,
        ],
        compiler_params=pltpu.CompilerParams(
            collective_id=0, has_side_effects=True, vmem_limit_bytes=40 * 1024 * 1024
        ),
        cost_estimate=pl.CostEstimate(
            flops=4 * (n_near + n_far) * rhs * width * width,
            bytes_accessed=2 * (near.size + left.size + right.size),
            transcendentals=0,
        ),
    )(*operands)
    return out.reshape(x_field.shape)


def solution(mesh):
    placed = (
        P("crow", "ccol", "lvl", None, None),
        P("crow", "ccol", "lvl", None, None, None),
        P("crow", "ccol", "lvl", None, None),
        P("crow", "ccol", "lvl", None, None, None),
        P("crow", "ccol", "lvl", None, None, None),
        P("crow", "ccol", "lvl", None, None),
        P("crow", "ccol", "lvl", None),
    )
    return jax.shard_map(
        per_device,
        mesh=mesh,
        in_specs=placed,
        out_specs=P("crow", "ccol", "lvl", None, None),
        check_vma=False,
    )
```

time: 37.9 us -> 28 us (0.74)
  Pallas kernels: 36.4 us -> 27.3 us
  local copies, waits for them, and re-layouts: 1.32 us -> 0.61 us
    pallas_call x1, Pallas kernels: 36.4 us -> 27.3 us  [per_device(): pl.pallas_call(functools.partial(kernel, n_row, n_col, n_lvl), out_shape=...]
    unnamed x1, local copies, waits for them, and re-layouts: 1.32 us -> 0.61 us
where the time goes in v2:
time: 28 us
  Pallas kernels  27.3 us (98%)
  local copies, waits for them, and re-layouts  0.61 us (2%)
    pallas_call x1, Pallas kernels, per_device(): pl.pallas_call(functools.partial(kernel, n_row, n_col, n_lvl), out_shape=...  27.3 us
    unnamed x1, local copies, waits for them, and re-layouts  0.61 us

profile of v2, /device:TPU:1, one launch (start us, length us, event | category | flops | bytes accessed | tf_op | source)
XLA Modules:
  0.0 28.0 jit_solution(3329601401138639823)
XLA Ops:
  0.0 27.3 %shard_map.73 = f32[16,256]{1,0:T(8,128)S(1)} custom-call(bf16[16,256]{1,0:T(8,128)(2,1)} %bitcast.18, bf16[64,256,256]{2,1,0:T(8,128)(2,1)} %bitcast.15, bf16[16,256,256]{2,1,0:T(8,128)(2,1)} %bitcast.16, bf16[16,256,256]{2,1,0:T(8,128)(2,1)} %bitcast.17, s32[2,64]{1,0:T(2,128)} %bitcast.19, s32[2,128]{1,0:T(2,128)} %bitcast.20, s32[2]{0:T(128)} %bitcast.21), custom_call_target="tpu_custom_call" | custom-call | flops 402653184 | bytes 12582912 | tf_op jit(solution)/shard_map/pallas_call | solution.py:254
  27.4 0.6 %copy.10 = f32[1,2,1,8,256]{4,3,2,1,0:T(8,128)} copy(f32[1,2,1,8,256]{4,3,2,1,0:T(8,128)S(1)} %bitcast.14) | data formatting | bytes 32768

commit v3 on v2

--- a/solution.py
+++ b/solution.py
@@ -9,7 +9,9 @@
 
 TILE = 4
 GROUP = 8
-UNROLL = 32
+CHUNK = 4
+LAG = 1
+EARLY = 2
 F32 = jnp.float32
 BF16 = jnp.bfloat16
 MESH = pl.DeviceIdType.MESH
@@ -40,7 +42,7 @@
     near, left, right, near_t, left_t, right_t,
     row_in, col_in, row_x, col_x, row_n, row_f, col_n, col_f,
     row_out, col_out, row_back, col_back,
-    small_sem, far_sem, near_sem, tab_sem, gsend, grow, gcol, rsend, rrow, rcol,
+    small_sem, far_sem, near_sem, tab_sem, gsend, grow, gcol, rsend, rrow, rcol, ready,
 ):
     r, c, k = lax.axis_index("crow"), lax.axis_index("ccol"), lax.axis_index("lvl")
     rhs, width = 8, x_ref.shape[1]
@@ -72,8 +74,15 @@
                 col_peers.append((to * n_lvl + ks[ok], {"crow": to, "ccol": c, "lvl": ks[ok]}))
 
     barrier = pltpu.get_barrier_semaphore()
-    for _, where in row_peers + col_peers:
-        pl.semaphore_signal(barrier, inc=1, device_id=where, device_id_type=MESH)
+    other = {"lvl": 1 - k}
+    for ahead, peers in ((0, col_peers), (1, row_peers)):
+        for at in range(0, len(peers) - 1, n_lvl):
+            where = {**peers[at][1], "lvl": jnp.int32(ahead)}
+            pl.semaphore_signal(barrier, inc=1, device_id=where, device_id_type=MESH)
+
+        @pl.when(k != ahead)
+        def _():
+            pl.semaphore_signal(barrier, inc=1, device_id=other, device_id_type=MESH)
 
     small = [
         pltpu.make_async_copy(src, dst, small_sem.at[i])
@@ -98,13 +107,31 @@
         near_copy(step).start()
 
     small[0].wait()
-    pl.semaphore_wait(barrier, rp - 1 + cp - 1)
-    for peers, buf, mine, sem in ((row_peers, row_in, me_r, grow), (col_peers, col_in, me_c, gcol)):
+    def meet_and_send(ahead, peers, buf, mine, sem):
+        @pl.when(k == ahead)
+        def _():
+            pl.semaphore_wait(barrier, len(peers))
+            pl.semaphore_signal(ready, inc=1, device_id=other, device_id_type=MESH)
+
+        @pl.when(k != ahead)
+        def _():
+            pl.semaphore_wait(ready, 1)
+
         for _, where in peers:
             pltpu.make_async_remote_copy(
                 src_ref=x_ref, dst_ref=buf.at[mine], send_sem=gsend, recv_sem=sem,
                 device_id=where, device_id_type=MESH,
             ).start()
+
+    meet_cols = functools.partial(meet_and_send, 0, col_peers, col_in, me_c, gcol)
+    meet_rows = functools.partial(meet_and_send, 1, row_peers, row_in, me_r, grow)
+
+    @pl.when(c >= EARLY)
+    def _():
+        meet_rows()
+        meet_cols()
+
+    pl.when(c < EARLY)(meet_cols)
 
     row_in[me_r] = x_ref[...]
     col_in[me_c] = x_ref[...]
@@ -142,6 +169,7 @@
 
     lax.fori_loop(0, near_sem.shape[0], near_turn, 0)
     tab_copy.wait()
+    pl.when(c < EARLY)(meet_rows)
 
     def drain(buf, count, sem):
         part = buf.at[pl.ds(0, count)]
@@ -155,74 +183,79 @@
                     dst[a * 2 * n_lvl + jj * n_lvl + kk] = v[jj]
             return carry
 
-        lax.fori_loop(0, src.shape[0] // n_lvl, body, 0)
+        lax.fori_loop(0, src.shape[0] // n_lvl, body, 0, unroll=4)
 
     diag = (
         lax.broadcasted_iota(jnp.int32, (GROUP * rhs, width), 0) // rhs
         == lax.broadcasted_iota(jnp.int32, (GROUP * rhs, width), 1) // rank
     )
-    far_u = UNROLL * n_groups // n_near
-
     def one_way(field, side, blocks, first, second, near_sum, far_sum, chain):
-        def body(step, carry):
-            for u in range(UNROLL):
-                slot = step * UNROLL + u
-                v = field[np_s[side, slot]].astype(BF16)
-                part = jnp.dot(v, blocks[slot], preferred_element_type=F32)
-                near_sum[slot + 1] = part + near_sum[tab_s[chain, slot]]
-            for u in range(far_u):
-                g = step * far_u + u
-                v = jnp.concatenate([field[fp_s[side, g * GROUP + w]] for w in range(GROUP)], 0)
-                coef = jnp.dot(v.astype(BF16), first[g], preferred_element_type=F32)
-                coef = jnp.where(diag, coef, 0.0).astype(BF16)
-                part = jnp.dot(coef, second[g], preferred_element_type=F32)
-                for w in range(GROUP):
-                    slot = g * GROUP + w
-                    far_sum[slot + 1] = part[w * rhs : (w + 1) * rhs] + far_sum[tab_s[2 + chain, slot]]
-            return carry
-
-        lax.fori_loop(0, n_near // UNROLL, body, 0)
-
-    def collect(near_sum, far_sum, chain, out):
-        def body(a, carry):
-            for kk in range(n_lvl):
-                parts = []
-                for jj in range(2):
-                    p = a * 2 * n_lvl + jj * n_lvl + kk
-                    parts.append(near_sum[tab_s[4 + chain, p]] + far_sum[tab_s[6 + chain, p]])
-                out[a * n_lvl + kk] = jnp.concatenate(parts, 0).astype(BF16)
-            return carry
-
-        lax.fori_loop(0, out.shape[0] // n_lvl, body, 0)
-
-    def send_back(peers, src, dst, mine, sem):
-        for to, where in peers:
-            pltpu.make_async_remote_copy(
-                src_ref=src.at[to], dst_ref=dst.at[mine], send_sem=rsend, recv_sem=sem,
-                device_id=where, device_id_type=MESH,
-            ).start()
+        every = n_near // n_groups
+
+        def coefficients(g):
+            v = jnp.concatenate([field[fp_s[side, g * GROUP + w]] for w in range(GROUP)], 0)
+            coef = jnp.dot(v.astype(BF16), first[g], preferred_element_type=F32)
+            return jnp.where(diag, coef, 0.0).astype(BF16)
+
+        def near_slot(slot):
+            v = field[np_s[side, slot]].astype(BF16)
+            part = jnp.dot(v, blocks[slot], preferred_element_type=F32)
+            near_sum[slot + 1] = part + near_sum[tab_s[chain, slot]]
+
+        def far_group(g, coef):
+            part = jnp.dot(coef, second[g], preferred_element_type=F32)
+            for w in range(GROUP):
+                slot = g * GROUP + w
+                far_sum[slot + 1] = part[w * rhs : (w + 1) * rhs] + far_sum[tab_s[2 + chain, slot]]
+
+        coefs = {}
+        for g in range(n_groups + LAG):
+            if g < n_groups:
+                coefs[g] = coefficients(g)
+                for slot in range(g * every, (g + 1) * every):
+                    near_slot(slot)
+            if g >= LAG:
+                far_group(g - LAG, coefs.pop(g - LAG))
+
+    def collect(near_sum, far_sum, chain, out, to):
+        first = 2 * n_lvl * (to // n_lvl) + lax.rem(to, n_lvl)
+        parts = []
+        for jj in range(2):
+            p = first + jj * n_lvl
+            parts.append(near_sum[tab_s[4 + chain, p]] + far_sum[tab_s[6 + chain, p]])
+        out[to] = jnp.concatenate(parts, 0).astype(BF16)
+
+    def give_back(src, dst, mine, sem, to, where):
+        pltpu.make_async_remote_copy(
+            src_ref=src.at[to], dst_ref=dst.at[mine], send_sem=rsend, recv_sem=sem,
+            device_id=where, device_id_type=MESH,
+        ).start()
+
+    def give_all(near_sum, far_sum, chain, peers, src, dst, mine, sem):
+        for at in range(0, len(peers), CHUNK):
+            for to, _ in peers[at : at + CHUNK]:
+                collect(near_sum, far_sum, chain, src, to)
+            for peer in peers[at : at + CHUNK]:
+                give_back(src, dst, mine, sem, *peer)
+        collect(near_sum, far_sum, chain, dst, mine)
+
+    drain(col_in, cp - 1, gcol)
+    unpack(col_in, col_x)
+    one_way(col_x, 1, near_t, right_t, left, row_n, row_f, 0)
+    give_all(row_n, row_f, 0, row_peers, row_out, row_back, me_r, rrow)
 
     drain(row_in, rp - 1, grow)
     unpack(row_in, row_x)
     one_way(row_x, 0, near, left_t, right, col_n, col_f, 1)
-    collect(col_n, col_f, 1, col_out)
-    send_back(col_peers, col_out, col_back, me_c, rcol)
-
-    drain(col_in, cp - 1, gcol)
-    unpack(col_in, col_x)
-    one_way(col_x, 1, near_t, right_t, left, row_n, row_f, 0)
-    collect(row_n, row_f, 0, row_out)
-    send_back(row_peers, row_out, row_back, me_r, rrow)
-
-    col_back[me_c] = col_out[me_c]
-    row_back[me_r] = row_out[me_r]
+    give_all(col_n, col_f, 1, col_peers, col_out, col_back, me_c, rcol)
+
+    drain(row_back, rp - 1, rrow)
+    total = row_back[0].astype(F32)
+    for a in range(1, rp):
+        total = total + row_back[a].astype(F32)
     drain(col_back, cp - 1, rcol)
-    total = col_back[0].astype(F32)
-    for a in range(1, cp):
+    for a in range(cp):
         total = total + col_back[a].astype(F32)
-    drain(row_back, rp - 1, rrow)
-    for a in range(rp):
-        total = total + row_back[a].astype(F32)
     out_ref[...] = total
     drain(row_in, rp - 1, gsend)
     drain(col_in, cp - 1, gsend)
@@ -287,6 +320,7 @@
             dma((2,)),
             dma((8,)),
             dma, dma, dma, dma, dma, dma, dma,
+            pltpu.SemaphoreType.REGULAR,
         ],
         compiler_params=pltpu.CompilerParams(
             collective_id=0, has_side_effects=True, vmem_limit_bytes=40 * 1024 * 1024

time: 28 us -> 25.9 us (0.925)
  Pallas kernels: 27.3 us -> 25.2 us
    pallas_call x1, Pallas kernels: 27.3 us -> 25.2 us  [per_device(): pl.pallas_call(functools.partial(kernel, n_row, n_col, n_lvl), out_shape=...]
where the time goes in v3:
time: 25.9 us; the launch traced here: 25.8 us
  Pallas kernels  25.2 us (97%)
  local copies, waits for them, and re-layouts  0.61 us (2%)
    pallas_call x1, Pallas kernels, per_device(): pl.pallas_call(functools.partial(kernel, n_row, n_col, n_lvl), out_shape=...  25.2 us
    unnamed x1, local copies, waits for them, and re-layouts  0.61 us

profile of v3, /device:TPU:1, one launch (start us, length us, event | category | flops | bytes accessed | tf_op | source)
XLA Modules:
  0.0 25.8 jit_solution(8266633509783641020)
XLA Ops:
  0.0 25.2 %shard_map.73 = f32[16,256]{1,0:T(8,128)S(1)} custom-call(bf16[16,256]{1,0:T(8,128)(2,1)} %bitcast.18, bf16[64,256,256]{2,1,0:T(8,128)(2,1)} %bitcast.15, bf16[16,256,256]{2,1,0:T(8,128)(2,1)} %bitcast.16, bf16[16,256,256]{2,1,0:T(8,128)(2,1)} %bitcast.17, s32[2,64]{1,0:T(2,128)} %bitcast.19, s32[2,128]{1,0:T(2,128)} %bitcast.20, s32[2]{0:T(128)} %bitcast.21), custom_call_target="tpu_custom_call" | custom-call | flops 402653184 | bytes 12582912 | tf_op jit(solution)/shard_map/pallas_call | solution.py:287
  25.2 0.6 %copy.10 = f32[1,2,1,8,256]{4,3,2,1,0:T(8,128)} copy(f32[1,2,1,8,256]{4,3,2,1,0:T(8,128)S(1)} %bitcast.14) | data formatting | bytes 32768

commit v4 on v3

--- a/solution.py
+++ b/solution.py
@@ -11,7 +11,7 @@
 GROUP = 8
 CHUNK = 4
 LAG = 1
-EARLY = 2
+STAGES = (3, 2, 1, 0)
 F32 = jnp.float32
 BF16 = jnp.bfloat16
 MESH = pl.DeviceIdType.MESH
@@ -60,11 +60,12 @@
     ys = [y] + [lax.rem(y + o, ny) for o in range(1, ny)]
     xs = [x] + [lax.rem(x + o, nx) for o in range(1, nx)]
     ks = [k] + [lax.rem(k + o, n_lvl) for o in range(1, n_lvl)]
-    row_peers, col_peers = [], []
+    row_peers, col_peers, row_far, col_far = [], [], [], []
     for oz in far_first(n_col):
         for ok in range(n_lvl):
             if oz or ok:
                 row_peers.append((zs[oz] * n_lvl + ks[ok], {"crow": r, "ccol": zs[oz], "lvl": ks[ok]}))
+                row_far.append(min(oz, n_col - oz))
     grid = [(oy, ox) for oy in range(ny) for ox in range(nx)]
     grid.sort(key=lambda o: -min(o[0], ny - o[0]) - min(o[1], nx - o[1]))
     for oy, ox in grid:
@@ -72,11 +73,12 @@
         for ok in range(n_lvl):
             if oy or ox or ok:
                 col_peers.append((to * n_lvl + ks[ok], {"crow": to, "ccol": c, "lvl": ks[ok]}))
+                col_far.append(min(oy, ny - oy) + min(ox, nx - ox))
 
     barrier = pltpu.get_barrier_semaphore()
     other = {"lvl": 1 - k}
     for ahead, peers in ((0, col_peers), (1, row_peers)):
-        for at in range(0, len(peers) - 1, n_lvl):
+        for at in reversed(range(0, len(peers) - 1, n_lvl)):
             where = {**peers[at][1], "lvl": jnp.int32(ahead)}
             pl.semaphore_signal(barrier, inc=1, device_id=where, device_id_type=MESH)
 
@@ -107,7 +109,7 @@
         near_copy(step).start()
 
     small[0].wait()
-    def meet_and_send(ahead, peers, buf, mine, sem):
+    def meet(ahead, peers):
         @pl.when(k == ahead)
         def _():
             pl.semaphore_wait(barrier, len(peers))
@@ -117,22 +119,38 @@
         def _():
             pl.semaphore_wait(ready, 1)
 
-        for _, where in peers:
-            pltpu.make_async_remote_copy(
-                src_ref=x_ref, dst_ref=buf.at[mine], send_sem=gsend, recv_sem=sem,
-                device_id=where, device_id_type=MESH,
-            ).start()
-
-    meet_cols = functools.partial(meet_and_send, 0, col_peers, col_in, me_c, gcol)
-    meet_rows = functools.partial(meet_and_send, 1, row_peers, row_in, me_r, grow)
-
-    @pl.when(c >= EARLY)
-    def _():
-        meet_rows()
-        meet_cols()
-
-    pl.when(c < EARLY)(meet_cols)
-
+    def give_x(where, buf, mine, sem):
+        pltpu.make_async_remote_copy(
+            src_ref=x_ref, dst_ref=buf.at[mine], send_sem=gsend, recv_sem=sem,
+            device_id=where, device_id_type=MESH,
+        ).start()
+
+    def meet_cols():
+        meet(0, col_peers)
+        for _, where in col_peers:
+            give_x(where, col_in, me_c, gcol)
+
+    def meet_rows():
+        meet(1, row_peers)
+        for _, where in row_peers:
+            give_x(where, row_in, me_r, grow)
+
+    def meet_both():
+        meet(0, col_peers)
+        meet(1, row_peers)
+        todo = [(far, where, col_in, me_c, gcol) for far, (_, where) in zip(col_far, col_peers)]
+        todo += [(far, where, row_in, me_r, grow) for far, (_, where) in zip(row_far, row_peers)]
+        for _, *args in sorted(todo, key=lambda item: -item[0]):
+            give_x(*args)
+
+    def rows_at(stage):
+        for plane, at in enumerate(STAGES):
+            if at == stage:
+                pl.when(c == plane)(meet_rows)
+
+    pl.when(c >= len(STAGES))(meet_both)
+    pl.when(c < len(STAGES))(meet_cols)
+    rows_at(0)
     row_in[me_r] = x_ref[...]
     col_in[me_c] = x_ref[...]
     for copy in small[1:]:
@@ -158,7 +176,8 @@
         right_t[g] = right[g].T
         return carry
 
-    lax.fori_loop(0, n_groups, far_turn, 0)
+    lax.fori_loop(0, n_groups, far_turn, 0, unroll=4)
+    rows_at(1)
 
     def near_turn(step, carry):
         near_copy(step).wait()
@@ -167,9 +186,14 @@
             near_t[slot] = near[slot].T
         return carry
 
-    lax.fori_loop(0, near_sem.shape[0], near_turn, 0)
+    steps = near_sem.shape[0]
+    lax.fori_loop(0, steps // 2, near_turn, 0)
+    rows_at(2)
+    lax.fori_loop(steps // 2, 3 * steps // 4, near_turn, 0)
+    rows_at(3)
+    lax.fori_loop(3 * steps // 4, steps, near_turn, 0)
     tab_copy.wait()
-    pl.when(c < EARLY)(meet_rows)
+    rows_at(4)
 
     def drain(buf, count, sem):
         part = buf.at[pl.ds(0, count)]
@@ -183,7 +207,7 @@
                     dst[a * 2 * n_lvl + jj * n_lvl + kk] = v[jj]
             return carry
 
-        lax.fori_loop(0, src.shape[0] // n_lvl, body, 0, unroll=4)
+        lax.fori_loop(0, src.shape[0] // n_lvl, body, 0, unroll=8)
 
     diag = (
         lax.broadcasted_iota(jnp.int32, (GROUP * rhs, width), 0) // rhs

time: 25.9 us -> 25.2 us (0.973)
  Pallas kernels: 25.2 us -> 24.5 us
    pallas_call x1, Pallas kernels: 25.2 us -> 24.5 us  [per_device(): pl.pallas_call(functools.partial(kernel, n_row, n_col, n_lvl), out_shape=...]
where the time goes in v4:
time: 25.2 us; the launch traced here: 25.1 us
  Pallas kernels  24.5 us (97%)
  local copies, waits for them, and re-layouts  0.61 us (2%)
    pallas_call x1, Pallas kernels, per_device(): pl.pallas_call(functools.partial(kernel, n_row, n_col, n_lvl), out_shape=...  24.5 us
    unnamed x1, local copies, waits for them, and re-layouts  0.61 us

profile of v4, /device:TPU:1, one launch (start us, length us, event | category | flops | bytes accessed | tf_op | source)
XLA Modules:
  0.0 25.1 jit_solution(16007746971972519969)
XLA Ops:
  0.0 24.5 %shard_map.73 = f32[16,256]{1,0:T(8,128)S(1)} custom-call(bf16[16,256]{1,0:T(8,128)(2,1)} %bitcast.18, bf16[64,256,256]{2,1,0:T(8,128)(2,1)} %bitcast.15, bf16[16,256,256]{2,1,0:T(8,128)(2,1)} %bitcast.16, bf16[16,256,256]{2,1,0:T(8,128)(2,1)} %bitcast.17, s32[2,64]{1,0:T(2,128)} %bitcast.19, s32[2,128]{1,0:T(2,128)} %bitcast.20, s32[2]{0:T(128)} %bitcast.21), custom_call_target="tpu_custom_call" | custom-call | flops 402653184 | bytes 12582912 | tf_op jit(solution)/shard_map/pallas_call | solution.py:311
  24.5 0.6 %copy.10 = f32[1,2,1,8,256]{4,3,2,1,0:T(8,128)} copy(f32[1,2,1,8,256]{4,3,2,1,0:T(8,128)S(1)} %bitcast.14) | data formatting | bytes 32768

commit v5 on v4

--- a/solution.py
+++ b/solution.py
@@ -9,7 +9,7 @@
 
 TILE = 4
 GROUP = 8
-CHUNK = 4
+CHUNK = 8
 LAG = 1
 STAGES = (3, 2, 1, 0)
 F32 = jnp.float32
@@ -273,16 +273,18 @@
     one_way(row_x, 0, near, left_t, right, col_n, col_f, 1)
     give_all(col_n, col_f, 1, col_peers, col_out, col_back, me_c, rcol)
 
-    drain(row_back, rp - 1, rrow)
-    total = row_back[0].astype(F32)
-    for a in range(1, rp):
-        total = total + row_back[a].astype(F32)
-    drain(col_back, cp - 1, rcol)
-    for a in range(cp):
-        total = total + col_back[a].astype(F32)
-    out_ref[...] = total
+    def added(parts):
+        while len(parts) > 1:
+            odd = parts[-1:] if len(parts) % 2 else []
+            parts = [p + q for p, q in zip(parts[::2], parts[1::2])] + odd
+        return parts[0]
+
     drain(row_in, rp - 1, gsend)
     drain(col_in, cp - 1, gsend)
+    drain(row_back, rp - 1, rrow)
+    total = added([row_back[a].astype(F32) for a in range(rp)])
+    drain(col_back, cp - 1, rcol)
+    out_ref[...] = total + added([col_back[a].astype(F32) for a in range(cp)])
     drain(row_back, rp - 1, rsend)
     drain(col_back, cp - 1, rsend)
 

time: 25.2 us -> 25.2 us (level)
  no operation moved by 1% of the time
where the time goes in v5:
time: 25.2 us
  Pallas kernels  24.5 us (97%)
  local copies, waits for them, and re-layouts  0.61 us (2%)
    pallas_call x1, Pallas kernels, per_device(): pl.pallas_call(functools.partial(kernel, n_row, n_col, n_lvl), out_shape=...  24.5 us
    unnamed x1, local copies, waits for them, and re-layouts  0.61 us

profile of v5, /device:TPU:1, one launch (start us, length us, event | category | flops | bytes accessed | tf_op | source)
XLA Modules:
  0.0 25.2 jit_solution(4040983020464982902)
XLA Ops:
  0.0 24.5 %shard_map.73 = f32[16,256]{1,0:T(8,128)S(1)} custom-call(bf16[16,256]{1,0:T(8,128)(2,1)} %bitcast.18, bf16[64,256,256]{2,1,0:T(8,128)(2,1)} %bitcast.15, bf16[16,256,256]{2,1,0:T(8,128)(2,1)} %bitcast.16, bf16[16,256,256]{2,1,0:T(8,128)(2,1)} %bitcast.17, s32[2,64]{1,0:T(2,128)} %bitcast.19, s32[2,128]{1,0:T(2,128)} %bitcast.20, s32[2]{0:T(128)} %bitcast.21), custom_call_target="tpu_custom_call" | custom-call | flops 402653184 | bytes 12582912 | tf_op jit(solution)/shard_map/pallas_call | solution.py:313
  24.6 0.6 %copy.10 = f32[1,2,1,8,256]{4,3,2,1,0:T(8,128)} copy(f32[1,2,1,8,256]{4,3,2,1,0:T(8,128)S(1)} %bitcast.14) | data formatting | bytes 32768
